TPU v7x, 512 devices: a whole 4x8x8 slice. The times are simulated.
512 devices in a mesh: mp: 128 (over x, y_hi, z, core), tok: 4 (over y_lo).
Axes of the slice: x: 4, y: 8 (y_hi: 2, y_lo: 4; y = y_hi * 4 + y_lo), z: 8, core: 2. Of those that a mesh axis runs over, the one named last changes fastest.
Arguments:
- tokens: bfloat16 [896, 4096], P('tok'), may hold values from -6 to 6
- gate_weight: bfloat16 [49152, 4096], P('mp', 'tok'), may hold values from -6 to 6
- up_weight: bfloat16 [49152, 4096], P('mp', 'tok'), may hold values from -6 to 6
- pair_list: int32 [16], replicated, may hold values from 0 to 15, each once
- unit_perm: int32 [16, 1536], replicated, may hold values from 0 to 1535, each once within a row
Outputs:
- merged_gate: bfloat16 [49152, 4096], P('mp', 'tok')
- merged_up: bfloat16 [49152, 4096], P('mp', 'tok')
- correlation: bfloat16 [49152, 768], P('mp', 'tok')
Inputs may be any that keep to these rules, and one draw needn't show every extreme that they name: pair_list is a permutation of the 16 slots. Each row of unit_perm is a permutation of the 1536 hidden units.
All inputs are finite; a program needn't handle non-finite values.
Results may differ from a plain program's by a relative error of at most 0.0057.
Values may be sent and summed in bfloat16 or wider, within the bound.
A program may use at most 64 MiB of HBM per device.

v0:
```python
import jax
import jax.numpy as jnp
from jax import lax
from jax.experimental import pallas as pl
from jax.experimental.pallas import tpu as pltpu
from jax.sharding import PartitionSpec as P

GROUP = 4
TOK = 4
MESH = pl.DeviceIdType.MESH
BF16 = jnp.bfloat16
F32 = jnp.float32


def kernel(
    gate_ref, up_ref, tokens_ref, row_ref, col_ref, table_ref,
    fetched_ref, corr_ref,
    onehot, everyone, spread, chosen, mine, theirs, hidden, hid_chosen, collected, ordered,
    row_units, col_units, outgoing,
    y_send, y_recv, x_send, x_recv, core_send, core_recv, one_send, one_recv, two_send, two_recv,
    half_send, half_recv, rows_send, rows_recv, cols_recv, twin_send, twin_recv,
    pe_send, pe_recv, corr_send, corr_recv,
):
    mp = lax.axis_index("mp")
    tok = lax.axis_index("tok")
    core = mp % 2
    z = (mp // 2) % 8
    y_hi = (mp // 16) % 2
    x = mp // 32
    slots = spread.shape[1]
    band = spread.shape[2]
    rows, model_cols = gate_ref.shape
    tok_rows = tokens_ref.shape[0]
    lanes = tok_rows * TOK
    model = x // 2
    slot = (mp // GROUP) % slots
    piece = mp % GROUP
    z_bit = z % 2
    relay = z % 4 != 3
    z_at = (z // 4) * 3 + z % 4
    relay_model = lax.rem(x + tok, 2)
    relay_piece = lax.rem(x + 2 * (tok // 2) + z_at, GROUP)
    relay_half = relay_piece // 2
    band_at = (y_hi * 2 + tok // 2) * 6 + z_at
    rho = relay_piece * (gate_ref.shape[0] // spread.shape[2]) + band_at

    def position(x_, y_hi_, z_, core_):
        return ((x_ * 2 + y_hi_) * 8 + z_) * 2 + core_

    def member(side, s, z_bit_, core_):
        return ((side * slots + s) * 2 + z_bit_) * 2 + core_

    twin = (mp + 1 - 2 * core, tok)

    def along_y(step):
        there = tok + step
        wraps = jnp.logical_or(there < 0, there >= TOK)
        return jnp.where(wraps, mp + 16 * (1 - 2 * y_hi), mp), lax.rem(there + TOK, TOK)

    def remote(src, dst, send, recv, who):
        return pltpu.make_async_remote_copy(
            src_ref=src, dst_ref=dst, send_sem=send, recv_sem=recv, device_id=who, device_id_type=MESH
        )

    def move(src, dst, send, recv, who):
        itself = jnp.logical_and(who[0] == mp, who[1] == tok)

        @pl.when(jnp.logical_not(itself))
        def _():
            remote(src, dst, send, recv, who).start()

        @pl.when(itself)
        def _():
            pltpu.make_async_copy(src, dst, recv).start()

    def arrived(dst, recv):
        remote(dst, dst, recv, recv, twin).wait_recv()

    def left(src, send):
        remote(src, src, send, send, twin).wait_send()

    def loop(count, fn):
        lax.fori_loop(0, count, lambda i, c: (fn(i), c)[1], 0)

    def cols_of(i):
        return pl.ds(pl.multiple_of(i * model_cols, 128), model_cols)

    half_rows = pl.ds(pl.multiple_of(core * (tok_rows // 2), 16), tok_rows // 2)
    far = jnp.where(core == 1, 2, -2)
    sources = (lax.rem(tok + 3, TOK), lax.rem(tok + 1, TOK), lax.rem(tok + 2, TOK))

    @pl.when(relay)
    def _():
        for i, step in enumerate((1, -1, far)):
            who = along_y(step)
            remote(
                tokens_ref.at[half_rows, cols_of(x)], everyone.at[tok, half_rows, cols_of(x)],
                y_send.at[i], y_recv.at[i], who,
            ).start()

    per_piece = rows // band
    weights = (gate_ref, up_ref)

    def spread_band(i):
        j = lax.rem(i * 5 + ((slot * 4 + tok) * 3) // 8 + piece * 6, per_piece)
        zi = lax.rem(j, 6)
        h = lax.rem(j // 6, 2)
        xi = lax.rem(piece + 12 - 2 * h - zi, 4)
        there = position(xi, j // 12, (zi // 3) * 4 + lax.rem(zi, 3), 0)
        tok_at = 2 * h + lax.rem(model + xi, 2)
        at = pl.ds(pl.multiple_of(j * band, band), band)
        for a in range(2):
            move(weights[a].at[at, :], spread.at[tok, slot], one_send, one_recv, (there + a, tok_at))

    loop(per_piece, spread_band)

    @pl.when(relay)
    def _():
        everyone[tok] = tokens_ref[...]

    forward = model == 0
    block = 128
    lane_id = lax.broadcasted_iota(jnp.int32, (1, onehot.shape[1]), 1)
    right = jnp.where(forward, lane_id, row_ref[...])

    def fill(i):
        at = pl.ds(pl.multiple_of(i * block, block), block)
        unit_id = lax.broadcasted_iota(jnp.int32, (block, 1), 0) + i * block
        lhs = jnp.where(forward, col_ref[at, :], unit_id)
        onehot[at, :] = jnp.where(lhs == right, 1.0, 0.0).astype(BF16)

    loop(onehot.shape[0] // block, fill)

    @pl.when(relay)
    def _():
        for i, t in enumerate(sources):
            arrived(everyone.at[0, half_rows, cols_of(0)], y_recv.at[i])
            for d in range(1, 4):
                part = everyone.at[t, half_rows, cols_of(x)]
                remote(
                    part, part, x_send.at[i, d], x_recv.at[i, d],
                    (position(lax.rem(x + d, 4), y_hi, z, core), tok),
                ).start()

        arrived(spread, one_recv)

        def second(i):
            t = lax.rem(i + slot, slots)
            chosen[:, t] = spread[:, table_ref[relay_model, t]]
            for d in range(TOK):
                to = lax.rem(tok + d, TOK)
                for h in range(2):
                    move(
                        chosen.at[to, t, :, pl.ds(h * (model_cols // 2), model_cols // 2)],
                        collected.at[pl.ds(pl.multiple_of(rho * band, band), band), :],
                        two_send, two_recv, (member(1 - relay_model, t, h, core), to),
                    )

        loop(slots, second)

        for i, t in enumerate(sources):
            for d in range(1, 4):
                arrived(everyone.at[0, half_rows, cols_of(0)], x_recv.at[i, d])
            part = everyone.at[t, half_rows, :]
            remote(part, part, core_send.at[i], core_recv.at[i], twin).start()
        for i in range(3):
            arrived(everyone.at[0, half_rows, :], core_recv.at[i])

        def product(k):
            add = lax.dot_general(
                spread[k].reshape(slots * band, model_cols),
                everyone[:, :, cols_of(k)].reshape(lanes, model_cols),
                (((1,), (1,)), ((), ())), preferred_element_type=F32,
            )

            @pl.when(k == 0)
            def _():
                mine[...] = add

            @pl.when(k > 0)
            def _():
                mine[...] += add

        loop(TOK, product)
        remote(mine, theirs, half_send, half_recv, twin).start()
        arrived(theirs, half_recv)
        scale = (model_cols * TOK) ** (-0.5)

        def activate(s):
            at = pl.ds(pl.multiple_of(s * band, band), band)
            one, two = mine[at, :] * scale, theirs[at, :] * scale
            gate, up = jnp.where(core == 0, one, two), jnp.where(core == 0, two, one)
            hidden[s] = (gate / (1.0 + jnp.exp(-gate)) * up).astype(BF16)

        loop(slots, activate)

        @pl.when(relay_model == 0)
        def _():
            def send(i):
                t = lax.rem(i + slot, slots)
                hid_chosen[t] = hidden[jnp.where(core == 0, t, table_ref[0, t])]
                for d in range(2):
                    move(
                        hid_chosen.at[t], row_units.at[lax.rem(z_at, 2), band_at // 2],
                        rows_send, rows_recv,
                        (member(core, t, relay_half, lax.rem(z_at, 2)), lax.rem(relay_piece, 2) + 2 * d),
                    )

            loop(slots, send)

        @pl.when(relay_model == 1)
        def _():
            def send(i):
                t = core * (slots // 2) + lax.rem(i + slot, slots // 2)
                hid_chosen[t] = hidden[jnp.where(relay_half == 0, table_ref[1, t], t)]
                for h in range(2):
                    for d in range(2):
                        move(
                            hid_chosen.at[t], col_units.at[lax.rem(band_at, 12)],
                            rows_send, cols_recv,
                            (member(relay_half, t, h, y_hi), 2 * lax.rem(relay_piece, 2) + d),
                        )

            loop(slots // 2, send)

    arrived(collected, two_recv)
    half_cols = pl.ds(pl.multiple_of(z_bit * (model_cols // 2), 128), model_cols // 2)

    def order(i):
        r = lax.rem(piece + 2 + i, GROUP)
        at = pl.ds(pl.multiple_of(r * rows, 128), rows)
        value = jnp.dot(onehot[at, :], collected[...], preferred_element_type=F32).astype(BF16)

        @pl.when(r == piece)
        def _():
            fetched_ref[core, :, half_cols] = value

        @pl.when(r != piece)
        def _():
            ordered[r] = value
            remote(
                ordered.at[r], fetched_ref.at[core, :, half_cols], pe_send.at[r], pe_recv.at[piece],
                (member(model, slot, r // 2, lax.rem(r, 2)), tok),
            ).start()

    loop(GROUP, order)

    arrived(row_units.at[0], rows_recv)
    remote(row_units.at[core], row_units.at[core], twin_send, twin_recv, twin).start()
    arrived(col_units, cols_recv)
    arrived(row_units.at[0], twin_recv)
    cross = lax.dot_general(
        row_units[...].reshape(rows, lanes), col_units[...].reshape(rows // 2, lanes),
        (((1,), (1,)), ((), ())), preferred_element_type=F32,
    )
    cross = (cross * lanes ** (-0.5)).astype(BF16).reshape(2, rows // 32, 16, rows // 2)
    stays = core == lax.rem(tok, 2)

    @pl.when(stays)
    def _():
        for i in range(2):
            corr_ref[:, i] = cross[i]

    @pl.when(jnp.logical_not(stays))
    def _():
        for i in range(2):
            outgoing[:, i] = cross[i]
        remote(
            outgoing, corr_ref, corr_send, corr_recv,
            (member(model, slot, z_bit, lax.rem(tok, 2)), 2 * (tok // 2) + core),
        ).start()
        arrived(outgoing, corr_recv)
        left(outgoing, corr_send)

    for d in range(1, GROUP):
        c = lax.rem(piece + d, GROUP)
        arrived(ordered.at[0], pe_recv.at[c])
    for d in range(1, GROUP):
        c = lax.rem(piece + d, GROUP)
        left(ordered.at[0], pe_send.at[c])
    left(row_units.at[0], twin_send)

    keeps_one = relay & (relay_model == model) & (relay_piece == piece)
    loop(2 * per_piece - jnp.where(keeps_one, 1, 0), lambda i: left(spread.at[0, 0], one_send))

    @pl.when(relay)
    def _():
        for i in range(3):
            left(everyone.at[0, half_rows, cols_of(0)], y_send.at[i])
            left(everyone.at[0, half_rows, :], core_send.at[i])
            for d in range(1, 4):
                left(everyone.at[0, half_rows, cols_of(0)], x_send.at[i, d])
        left(mine, half_send)
        keeps_two = model == 1 - relay_model
        loop(
            2 * TOK * slots - jnp.where(keeps_two, 1, 0),
            lambda i: left(collected.at[pl.ds(0, band), :], two_send),
        )
        keeps_row = (
            (relay_model == 0) & (model == core) & (z_bit == relay_half)
            & (core == lax.rem(z_at, 2)) & (lax.rem(tok, 2) == lax.rem(relay_piece, 2))
        )
        keeps_col = (
            (relay_model == 1) & (model == relay_half) & (slot // (slots // 2) == core)
            & (core == y_hi) & (tok // 2 == lax.rem(relay_piece, 2))
        )
        loop(
            2 * slots - jnp.where(keeps_row | keeps_col, 1, 0),
            lambda i: left(hid_chosen.at[0], rows_send),
        )


def body(tokens, gate_weight, up_weight, pair_list, unit_perm):
    mp_size = lax.axis_size("mp")
    slots = pair_list.shape[0]
    rows, cols = gate_weight.shape
    tok_rows = tokens.shape[0]
    units = rows * GROUP
    lanes = tok_rows * TOK
    band = 16
    mp = lax.axis_index("mp")
    second = mp >= mp_size // 2
    slot = (mp // GROUP) % slots
    slot_ids = jnp.arange(slots, dtype=jnp.int32)
    inverse = jnp.sum(
        jnp.where(pair_list[None, :] == slot_ids[:, None], slot_ids[None, :], 0), axis=1
    )
    table = jnp.stack([inverse, pair_list])
    pair_index = jnp.where(second, inverse[slot], slot)
    order = lax.dynamic_index_in_dim(unit_perm, pair_index, 0, keepdims=False)
    vmem = pl.BlockSpec(memory_space=pltpu.VMEM)
    dma = pltpu.SemaphoreType.DMA
    fetched, cross = pl.pallas_call(
        kernel,
        out_shape=(
            jax.ShapeDtypeStruct((2, rows, cols), BF16),
            jax.ShapeDtypeStruct((rows // 32, 2, 16, rows // 2), BF16),
        ),
        in_specs=[vmem] * 5 + [pl.BlockSpec(memory_space=pltpu.SMEM)],
        out_specs=(vmem, vmem),
        scratch_shapes=[
            pltpu.VMEM((units, units), BF16),
            pltpu.VMEM((TOK, tok_rows, cols * TOK), BF16),
            pltpu.VMEM((TOK, slots, band, cols), BF16),
            pltpu.VMEM((TOK, slots, band, cols), BF16),
            pltpu.VMEM((slots * band, lanes), F32),
            pltpu.VMEM((slots * band, lanes), F32),
            pltpu.VMEM((slots, band, lanes), BF16),
            pltpu.VMEM((slots, band, lanes), BF16),
            pltpu.VMEM((units, cols // 2), BF16),
            pltpu.VMEM((GROUP, rows, cols // 2), BF16),
            pltpu.VMEM((2, rows // 32, band, lanes), BF16),
            pltpu.VMEM((rows // 32, band, lanes), BF16),
            pltpu.VMEM((rows // 32, 2, 16, rows // 2), BF16),
            dma((3,)), dma((3,)), dma((3, 4)), dma((3, 4)), dma((3,)), dma((3,)),
            dma, dma, dma, dma, dma, dma, dma, dma, dma, dma, dma,
            dma((GROUP,)), dma((GROUP,)), dma, dma,
        ],
        compiler_params=pltpu.CompilerParams(
            has_side_effects=True, vmem_limit_bytes=56 * 1024 * 1024
        ),
        cost_estimate=pl.CostEstimate(flops=4 * 10**9, bytes_accessed=10**7, transcendentals=10**5),
        name="merge",
    )(gate_weight, up_weight, tokens, order[None, :], order[:, None], table)
    signed = jnp.where(second, -1.0, 1.0)

    def merged(own, other):
        return ((own.astype(F32) + signed * other.astype(F32)) * 0.5).astype(BF16)

    correlation = cross.reshape(rows, rows // 2)
    return merged(gate_weight, fetched[0]), merged(up_weight, fetched[1]), correlation


def solution(mesh):
    in_specs = (P("tok", None), P("mp", "tok"), P("mp", "tok"), P(), P())
    out_specs = (P("mp", "tok"), P("mp", "tok"), P("mp", "tok"))
    return jax.shard_map(body, mesh=mesh, in_specs=in_specs, out_specs=out_specs, check_vma=False)
```

profile of v0, /device:TPU:313, one launch (start us, length us, event | category | flops | bytes accessed | tf_op | source)
XLA Modules:
  0.0 189.1 jit_solution(9329109421778565276)
XLA Ops:
  0.6 0.0 copy-start
  0.7 0.8 select_reduce_fusion
  1.5 0.6 dynamic_slice.7
  2.7 1.2 pad_add_fusion.table_ref
  3.9 0.0 copy-done
  3.9 0.6 constant_dynamic-slice_fusion.row_ref
  4.6 1.2 copy.11.col_ref
  5.7 0.0 copy-start.1
  5.7 0.0 copy-start.2
  5.7 179.3 %merge.1 = (bf16[2,384,1024]{2,1,0:T(8,128)(2,1)}, bf16[12,2,16,192]{3,2,1,0:T(8,128)(2,1)}) custom-call(bf16[384,1024]{1,0:T(8,128)(2,1)} %gate_ref.1, bf16[384,1024]{1,0:T(8,128)(2,1)} %up_ref.1, bf16[224,4096]{1,0:T(8,128)(2,1)} %tokens_ref.1, s32[1,1536]{1,0:T(1,128)} %constant_dynamic-slice_fusion.row_ref, s32[1536,1]{1,0:T(8,128)} %copy.11.col_ref, ...), custom_call_target="tpu_custom_call" | custom-call | flops 4000000000 | bytes 10000000 | tf_op jit(solution)/shard_map/merge/pallas_call | solution.py:333
  185.0 0.0 copy-done.1
  185.0 0.0 copy-done.2
  185.0 0.0 copy-start.3
  185.0 3.3 %fusion.1 = (bf16[384,1024]{1,0:T(8,128)(2,1)}, bf16[384,1024]{1,0:T(8,128)(2,1)}) fusion(bf16[384,1024]{1,0:T(8,128)(2,1)S(1)} %copy-done.1, bf16[2,384,1024]{2,1,0:T(8,128)(2,1)} %get-tuple-element.5, f32[]{:T(128)S(6)} %select_n.29, bf16[384,1024]{1,0:T(8,128)(2,1)S(1)} %copy-done.2), kind=kLoop, calls=%fused_computation.2 | loop fusion | flops 4718592 | bytes 4718596 | tf_op jit(solution)/shard_map/convert_element_type | solution.py:368
  188.3 0.0 copy-done.3
  188.3 0.8 copy.12
  (1 shorter events, 0.0 us)
Async XLA Ops:
  0.6 3.3 %copy-start = (s32[16,1536]{1,0:T(8,128)S(1)}, s32[16,1536]{1,0:T(8,128)}, u32[]{:S(2)}) copy-start(s32[16,1536]{1,0:T(8,128)} %param.9) | copy-start | bytes 294916
  5.7 179.3 %copy-start.1 = (bf16[384,1024]{1,0:T(8,128)(2,1)S(1)}, bf16[384,1024]{1,0:T(8,128)(2,1)}, u32[]{:S(2)}) copy-start(bf16[384,1024]{1,0:T(8,128)(2,1)} %up_ref.1) | copy-start | bytes 2359300
  5.7 179.3 %copy-start.2 = (bf16[384,1024]{1,0:T(8,128)(2,1)S(1)}, bf16[384,1024]{1,0:T(8,128)(2,1)}, u32[]{:S(2)}) copy-start(bf16[384,1024]{1,0:T(8,128)(2,1)} %gate_ref.1) | copy-start | bytes 2359300
  185.0 3.3 %copy-start.3 = (bf16[12,2,16,192]{3,2,1,0:T(8,128)(2,1)S(1)}, bf16[12,2,16,192]{3,2,1,0:T(8,128)(2,1)}, u32[]{:S(2)}) copy-start(bf16[12,2,16,192]{3,2,1,0:T(8,128)(2,1)} %get-tuple-element.6) | copy-start | bytes 442372
where the time goes:
time: 189 us
  Pallas kernels  179 us (95%)
  other arithmetic  5.29 us (3%)
  local copies, waits for them, and re-layouts  3.19 us (2%)
    pallas_call x1, Pallas kernels, body(): pl.pallas_call(kernel, out_shape=(jax.ShapeDtypeStruct((2, rows, cols), B...  179 us

commit v1 on v0

--- a/solution.py
+++ b/solution.py
@@ -1,3 +1,5 @@
+import functools
+
 import jax
 import jax.numpy as jnp
 from jax import lax
@@ -6,6 +8,7 @@
 from jax.sharding import PartitionSpec as P
 
 GROUP = 4
+STEPS = 2
 TOK = 4
 MESH = pl.DeviceIdType.MESH
 BF16 = jnp.bfloat16
@@ -13,13 +16,13 @@
 
 
 def kernel(
-    gate_ref, up_ref, tokens_ref, row_ref, col_ref, table_ref,
+    gate_ref, up_ref, tokens_ref, pair_ref, perm_ref,
     fetched_ref, corr_ref,
-    onehot, everyone, spread, chosen, mine, theirs, hidden, hid_chosen, collected, ordered,
-    row_units, col_units, outgoing,
+    onehot, everyone, mine, theirs, hidden, hid_chosen, row_units, col_units, outgoing, table_ref,
     y_send, y_recv, x_send, x_recv, core_send, core_recv, one_send, one_recv, two_send, two_recv,
     half_send, half_recv, rows_send, rows_recv, cols_recv, twin_send, twin_recv,
     pe_send, pe_recv, corr_send, corr_recv,
+    *parts,
 ):
     mp = lax.axis_index("mp")
     tok = lax.axis_index("tok")
@@ -27,8 +30,8 @@
     z = (mp // 2) % 8
     y_hi = (mp // 16) % 2
     x = mp // 32
-    slots = spread.shape[1]
-    band = spread.shape[2]
+    spread, chosen, collected, ordered = (parts[i * STEPS : (i + 1) * STEPS] for i in range(4))
+    slots, band, width = spread[0].shape[2:]
     rows, model_cols = gate_ref.shape
     tok_rows = tokens_ref.shape[0]
     lanes = tok_rows * TOK
@@ -42,7 +45,7 @@
     relay_piece = lax.rem(x + 2 * (tok // 2) + z_at, GROUP)
     relay_half = relay_piece // 2
     band_at = (y_hi * 2 + tok // 2) * 6 + z_at
-    rho = relay_piece * (gate_ref.shape[0] // spread.shape[2]) + band_at
+    rho = relay_piece * (rows // band) + band_at
 
     def position(x_, y_hi_, z_, core_):
         return ((x_ * 2 + y_hi_) * 8 + z_) * 2 + core_
@@ -98,10 +101,13 @@
                 y_send.at[i], y_recv.at[i], who,
             ).start()
 
+    def cols_part(h, step):
+        return pl.ds(h * (model_cols // 2) + step * width, width)
+
     per_piece = rows // band
     weights = (gate_ref, up_ref)
 
-    def spread_band(i):
+    def spread_band(step, i):
         j = lax.rem(i * 5 + ((slot * 4 + tok) * 3) // 8 + piece * 6, per_piece)
         zi = lax.rem(j, 6)
         h = lax.rem(j // 6, 2)
@@ -110,26 +116,38 @@
         tok_at = 2 * h + lax.rem(model + xi, 2)
         at = pl.ds(pl.multiple_of(j * band, band), band)
         for a in range(2):
-            move(weights[a].at[at, :], spread.at[tok, slot], one_send, one_recv, (there + a, tok_at))
-
-    loop(per_piece, spread_band)
+            for h in range(2):
+                move(
+                    weights[a].at[at, cols_part(h, step)], spread[step].at[tok, h, slot],
+                    one_send, one_recv.at[step], (there + a, tok_at),
+                )
+
+    for step in range(STEPS):
+        loop(per_piece, functools.partial(spread_band, step))
 
     @pl.when(relay)
     def _():
         everyone[tok] = tokens_ref[...]
+
+    def pairs_of(t):
+        def look(e, found):
+            return jnp.where(pair_ref[e] == t, e, found)
+
+        table_ref[0, t] = lax.fori_loop(0, slots, look, 0)
+        table_ref[1, t] = pair_ref[t]
+
+    loop(slots, pairs_of)
 
     forward = model == 0
     block = 128
     lane_id = lax.broadcasted_iota(jnp.int32, (1, onehot.shape[1]), 1)
-    right = jnp.where(forward, lane_id, row_ref[...])
-
-    def fill(i):
-        at = pl.ds(pl.multiple_of(i * block, block), block)
-        unit_id = lax.broadcasted_iota(jnp.int32, (block, 1), 0) + i * block
-        lhs = jnp.where(forward, col_ref[at, :], unit_id)
-        onehot[at, :] = jnp.where(lhs == right, 1.0, 0.0).astype(BF16)
-
-    loop(onehot.shape[0] // block, fill)
+    perm = perm_ref[pl.ds(jnp.where(forward, slot, table_ref[0, slot]), 1), :]
+    right = jnp.where(forward, lane_id, perm)
+    for i in range(onehot.shape[0] // block):
+        unit_id = lax.broadcasted_iota(jnp.int32, (block, block), 0) + i * block
+        down = jnp.broadcast_to(perm[:, i * block : (i + 1) * block], (block, block)).T
+        lhs = jnp.where(forward, down, unit_id)[:, :1]
+        onehot[pl.ds(i * block, block), :] = jnp.where(lhs == right, 1.0, 0.0).astype(BF16)
 
     @pl.when(relay)
     def _():
@@ -142,21 +160,21 @@
                     (position(lax.rem(x + d, 4), y_hi, z, core), tok),
                 ).start()
 
-        arrived(spread, one_recv)
-
-        def second(i):
+        def second(step, i):
             t = lax.rem(i + slot, slots)
-            chosen[:, t] = spread[:, table_ref[relay_model, t]]
+            chosen[step][:, :, t] = spread[step][:, :, table_ref[relay_model, t]]
             for d in range(TOK):
                 to = lax.rem(tok + d, TOK)
                 for h in range(2):
                     move(
-                        chosen.at[to, t, :, pl.ds(h * (model_cols // 2), model_cols // 2)],
-                        collected.at[pl.ds(pl.multiple_of(rho * band, band), band), :],
-                        two_send, two_recv, (member(1 - relay_model, t, h, core), to),
+                        chosen[step].at[to, h, t],
+                        collected[step].at[pl.ds(pl.multiple_of(rho * band, band), band), :],
+                        two_send, two_recv.at[step], (member(1 - relay_model, t, h, core), to),
                     )
 
-        loop(slots, second)
+        for step in range(STEPS):
+            arrived(spread[step], one_recv.at[step])
+            loop(slots, functools.partial(second, step))
 
         for i, t in enumerate(sources):
             for d in range(1, 4):
@@ -166,22 +184,21 @@
         for i in range(3):
             arrived(everyone.at[0, half_rows, :], core_recv.at[i])
 
-        def product(k):
+        def product(step, i):
+            k, h = i // 2, lax.rem(i, 2)
+            at = pl.ds(
+                pl.multiple_of(k * model_cols + h * (model_cols // 2) + step * width, 128), width
+            )
             add = lax.dot_general(
-                spread[k].reshape(slots * band, model_cols),
-                everyone[:, :, cols_of(k)].reshape(lanes, model_cols),
+                spread[step][k, h].reshape(slots * band, width),
+                everyone[:, :, at].reshape(lanes, width),
                 (((1,), (1,)), ((), ())), preferred_element_type=F32,
             )
-
-            @pl.when(k == 0)
-            def _():
-                mine[...] = add
-
-            @pl.when(k > 0)
-            def _():
-                mine[...] += add
-
-        loop(TOK, product)
+            mine[...] += add
+
+        mine[...] = jnp.zeros_like(mine)
+        for step in range(STEPS):
+            loop(2 * TOK, functools.partial(product, step))
         remote(mine, theirs, half_send, half_recv, twin).start()
         arrived(theirs, half_recv)
         scale = (model_cols * TOK) ** (-0.5)
@@ -223,13 +240,15 @@
 
             loop(slots // 2, send)
 
-    arrived(collected, two_recv)
-    half_cols = pl.ds(pl.multiple_of(z_bit * (model_cols // 2), 128), model_cols // 2)
-
-    def order(i):
+    def order(step, i):
+        half_cols = pl.ds(
+            pl.multiple_of(z_bit * (model_cols // 2) + step * width, 128), width
+        )
         r = lax.rem(piece + 2 + i, GROUP)
         at = pl.ds(pl.multiple_of(r * rows, 128), rows)
-        value = jnp.dot(onehot[at, :], collected[...], preferred_element_type=F32).astype(BF16)
+        value = jnp.dot(
+            onehot[at, :], collected[step][...], preferred_element_type=F32
+        ).astype(BF16)
 
         @pl.when(r == piece)
         def _():
@@ -237,13 +256,16 @@
 
         @pl.when(r != piece)
         def _():
-            ordered[r] = value
+            ordered[step][r] = value
             remote(
-                ordered.at[r], fetched_ref.at[core, :, half_cols], pe_send.at[r], pe_recv.at[piece],
+                ordered[step].at[r], fetched_ref.at[core, :, half_cols],
+                pe_send.at[step, r], pe_recv.at[step, piece],
                 (member(model, slot, r // 2, lax.rem(r, 2)), tok),
             ).start()
 
-    loop(GROUP, order)
+    for step in range(STEPS):
+        arrived(collected[step], two_recv.at[step])
+        loop(GROUP, functools.partial(order, step))
 
     arrived(row_units.at[0], rows_recv)
     remote(row_units.at[core], row_units.at[core], twin_send, twin_recv, twin).start()
@@ -272,16 +294,25 @@
         arrived(outgoing, corr_recv)
         left(outgoing, corr_send)
 
-    for d in range(1, GROUP):
-        c = lax.rem(piece + d, GROUP)
-        arrived(ordered.at[0], pe_recv.at[c])
-    for d in range(1, GROUP):
-        c = lax.rem(piece + d, GROUP)
-        left(ordered.at[0], pe_send.at[c])
+    for step in range(STEPS):
+        for d in range(1, GROUP):
+            c = lax.rem(piece + d, GROUP)
+            arrived(ordered[step].at[0], pe_recv.at[step, c])
+    for step in range(STEPS):
+        for d in range(1, GROUP):
+            c = lax.rem(piece + d, GROUP)
+            left(ordered[step].at[0], pe_send.at[step, c])
     left(row_units.at[0], twin_send)
 
     keeps_one = relay & (relay_model == model) & (relay_piece == piece)
-    loop(2 * per_piece - jnp.where(keeps_one, 1, 0), lambda i: left(spread.at[0, 0], one_send))
+    loop(
+        per_piece - jnp.where(keeps_one, 1, 0),
+        lambda i: [left(spread[0].at[0, 0, pl.ds(0, 2)], one_send) for _ in range(STEPS)],
+    )
+    loop(
+        per_piece,
+        lambda i: [left(spread[0].at[0, 0, pl.ds(0, 2)], one_send) for _ in range(STEPS)],
+    )
 
     @pl.when(relay)
     def _():
@@ -294,7 +325,7 @@
         keeps_two = model == 1 - relay_model
         loop(
             2 * TOK * slots - jnp.where(keeps_two, 1, 0),
-            lambda i: left(collected.at[pl.ds(0, band), :], two_send),
+            lambda i: [left(collected[0].at[pl.ds(0, band), :], two_send) for _ in range(STEPS)],
         )
         keeps_row = (
             (relay_model == 0) & (model == core) & (z_bit == relay_half)
@@ -320,14 +351,7 @@
     band = 16
     mp = lax.axis_index("mp")
     second = mp >= mp_size // 2
-    slot = (mp // GROUP) % slots
-    slot_ids = jnp.arange(slots, dtype=jnp.int32)
-    inverse = jnp.sum(
-        jnp.where(pair_list[None, :] == slot_ids[:, None], slot_ids[None, :], 0), axis=1
-    )
-    table = jnp.stack([inverse, pair_list])
-    pair_index = jnp.where(second, inverse[slot], slot)
-    order = lax.dynamic_index_in_dim(unit_perm, pair_index, 0, keepdims=False)
+    width = cols // 2 // STEPS
     vmem = pl.BlockSpec(memory_space=pltpu.VMEM)
     dma = pltpu.SemaphoreType.DMA
     fetched, cross = pl.pallas_call(
@@ -336,32 +360,32 @@
             jax.ShapeDtypeStruct((2, rows, cols), BF16),
             jax.ShapeDtypeStruct((rows // 32, 2, 16, rows // 2), BF16),
         ),
-        in_specs=[vmem] * 5 + [pl.BlockSpec(memory_space=pltpu.SMEM)],
+        in_specs=[vmem] * 3 + [pl.BlockSpec(memory_space=pltpu.SMEM), vmem],
         out_specs=(vmem, vmem),
         scratch_shapes=[
             pltpu.VMEM((units, units), BF16),
             pltpu.VMEM((TOK, tok_rows, cols * TOK), BF16),
-            pltpu.VMEM((TOK, slots, band, cols), BF16),
-            pltpu.VMEM((TOK, slots, band, cols), BF16),
             pltpu.VMEM((slots * band, lanes), F32),
             pltpu.VMEM((slots * band, lanes), F32),
             pltpu.VMEM((slots, band, lanes), BF16),
             pltpu.VMEM((slots, band, lanes), BF16),
-            pltpu.VMEM((units, cols // 2), BF16),
-            pltpu.VMEM((GROUP, rows, cols // 2), BF16),
             pltpu.VMEM((2, rows // 32, band, lanes), BF16),
             pltpu.VMEM((rows // 32, band, lanes), BF16),
             pltpu.VMEM((rows // 32, 2, 16, rows // 2), BF16),
+            pltpu.SMEM((2, slots), jnp.int32),
             dma((3,)), dma((3,)), dma((3, 4)), dma((3, 4)), dma((3,)), dma((3,)),
-            dma, dma, dma, dma, dma, dma, dma, dma, dma, dma, dma,
-            dma((GROUP,)), dma((GROUP,)), dma, dma,
+            dma, dma((STEPS,)), dma, dma((STEPS,)), dma, dma, dma, dma, dma, dma, dma,
+            dma((STEPS, GROUP)), dma((STEPS, GROUP)), dma, dma,
+            *[pltpu.VMEM((TOK, 2, slots, band, width), BF16)] * (2 * STEPS),
+            *[pltpu.VMEM((units, width), BF16)] * STEPS,
+            *[pltpu.VMEM((GROUP, rows, width), BF16)] * STEPS,
         ],
         compiler_params=pltpu.CompilerParams(
             has_side_effects=True, vmem_limit_bytes=56 * 1024 * 1024
         ),
         cost_estimate=pl.CostEstimate(flops=4 * 10**9, bytes_accessed=10**7, transcendentals=10**5),
         name="merge",
-    )(gate_weight, up_weight, tokens, order[None, :], order[:, None], table)
+    )(gate_weight, up_weight, tokens, pair_list, unit_perm)
     signed = jnp.where(second, -1.0, 1.0)
 
     def merged(own, other):

time: 189 us -> 169 us (0.89)
  the two profiles are of different devices: /device:TPU:313 before, /device:TPU:136 now
where the time goes in v1:
time: 169 us
  Pallas kernels  164 us (97%)
  other arithmetic  3.29 us (2%)
    pallas_call x1, Pallas kernels, body(): pl.pallas_call(kernel, out_shape=(jax.ShapeDtypeStruct((2, rows, cols), B...  164 us

profile of v1, /device:TPU:136, one launch (start us, length us, event | category | flops | bytes accessed | tf_op | source)
XLA Modules:
  0.0 169.2 jit_solution(7487141935188823887)
XLA Ops:
  0.6 0.0 copy-start
  0.6 0.0 copy-start.1
  0.7 164.4 %merge.1 = (bf16[2,384,1024]{2,1,0:T(8,128)(2,1)}, bf16[12,2,16,192]{3,2,1,0:T(8,128)(2,1)}) custom-call(bf16[384,1024]{1,0:T(8,128)(2,1)} %gate_ref.1, bf16[384,1024]{1,0:T(8,128)(2,1)} %up_ref.1, bf16[224,4096]{1,0:T(8,128)(2,1)} %tokens_ref.1, s32[16]{0:T(128)} %pair_ref.1, s32[16,1536]{1,0:T(8,128)} %perm_ref.1), custom_call_target="tpu_custom_call" | custom-call | flops 4000000000 | bytes 10000000 | tf_op jit(solution)/shard_map/merge/pallas_call | solution.py:357
  165.1 0.0 copy-done
  165.1 0.0 copy-done.1
  165.1 0.0 copy-start.2
  165.1 3.3 %fusion.1 = (bf16[384,1024]{1,0:T(8,128)(2,1)}, bf16[384,1024]{1,0:T(8,128)(2,1)}) fusion(bf16[384,1024]{1,0:T(8,128)(2,1)S(1)} %copy-done, bf16[2,384,1024]{2,1,0:T(8,128)(2,1)} %get-tuple-element.5, f32[]{:T(128)S(6)} %select_n.4, bf16[384,1024]{1,0:T(8,128)(2,1)S(1)} %copy-done.1), kind=kLoop, calls=%fused_computation.2 | loop fusion | flops 4718592 | bytes 4718596 | tf_op jit(solution)/shard_map/convert_element_type | solution.py:392
  168.4 0.0 copy-done.2
  168.4 0.8 copy.8
Async XLA Ops:
  0.6 164.5 %copy-start = (bf16[384,1024]{1,0:T(8,128)(2,1)S(1)}, bf16[384,1024]{1,0:T(8,128)(2,1)}, u32[]{:S(2)}) copy-start(bf16[384,1024]{1,0:T(8,128)(2,1)} %up_ref.1) | copy-start | bytes 2359300
  0.6 164.5 %copy-start.1 = (bf16[384,1024]{1,0:T(8,128)(2,1)S(1)}, bf16[384,1024]{1,0:T(8,128)(2,1)}, u32[]{:S(2)}) copy-start(bf16[384,1024]{1,0:T(8,128)(2,1)} %gate_ref.1) | copy-start | bytes 2359300
  165.1 3.3 %copy-start.2 = (bf16[12,2,16,192]{3,2,1,0:T(8,128)(2,1)S(1)}, bf16[12,2,16,192]{3,2,1,0:T(8,128)(2,1)}, u32[]{:S(2)}) copy-start(bf16[12,2,16,192]{3,2,1,0:T(8,128)(2,1)} %get-tuple-element.6) | copy-start | bytes 442372

commit v2 on v1

--- a/solution.py
+++ b/solution.py
@@ -360,7 +360,7 @@
             jax.ShapeDtypeStruct((2, rows, cols), BF16),
             jax.ShapeDtypeStruct((rows // 32, 2, 16, rows // 2), BF16),
         ),
-        in_specs=[vmem] * 3 + [pl.BlockSpec(memory_space=pltpu.SMEM), vmem],
+        in_specs=[pl.BlockSpec(memory_space=pl.ANY)] * 2 + [vmem, pl.BlockSpec(memory_space=pltpu.SMEM), vmem],
         out_specs=(vmem, vmem),
         scratch_shapes=[
             pltpu.VMEM((units, units), BF16),

time: 169 us -> 170 us (level)
  no operation moved by 1% of the time
where the time goes in v2:
time: 170 us; the launch traced here: 169 us
  Pallas kernels  165 us (97%)
  other arithmetic  3.29 us (2%)
    pallas_call x1, Pallas kernels, body(): pl.pallas_call(kernel, out_shape=(jax.ShapeDtypeStruct((2, rows, cols), B...  165 us

profile of v2, /device:TPU:136, one launch (start us, length us, event | category | flops | bytes accessed | tf_op | source)
XLA Modules:
  0.0 169.4 jit_solution(2913632700255081224)
XLA Ops:
  0.6 0.0 copy-start
  0.6 0.0 copy-start.1
  0.7 164.6 %merge.1 = (bf16[2,384,1024]{2,1,0:T(8,128)(2,1)}, bf16[12,2,16,192]{3,2,1,0:T(8,128)(2,1)}) custom-call(bf16[384,1024]{1,0:T(8,128)(2,1)} %gate_ref.1, bf16[384,1024]{1,0:T(8,128)(2,1)} %up_ref.1, bf16[224,4096]{1,0:T(8,128)(2,1)} %tokens_ref.1, s32[16]{0:T(128)} %pair_ref.1, s32[16,1536]{1,0:T(8,128)} %perm_ref.1), custom_call_target="tpu_custom_call" | custom-call | flops 4000000000 | bytes 10000000 | tf_op jit(solution)/shard_map/merge/pallas_call | solution.py:357
  165.3 0.0 copy-done
  165.3 0.0 copy-done.1
  165.3 0.0 copy-start.2
  165.3 3.3 %fusion.1 = (bf16[384,1024]{1,0:T(8,128)(2,1)}, bf16[384,1024]{1,0:T(8,128)(2,1)}) fusion(bf16[384,1024]{1,0:T(8,128)(2,1)S(1)} %copy-done, bf16[2,384,1024]{2,1,0:T(8,128)(2,1)} %get-tuple-element.5, f32[]{:T(128)S(6)} %select_n.4, bf16[384,1024]{1,0:T(8,128)(2,1)S(1)} %copy-done.1), kind=kLoop, calls=%fused_computation.2 | loop fusion | flops 4718592 | bytes 4718596 | tf_op jit(solution)/shard_map/convert_element_type | solution.py:392
  168.6 0.0 copy-done.2
  168.6 0.8 copy.8
Async XLA Ops:
  0.6 164.7 %copy-start = (bf16[384,1024]{1,0:T(8,128)(2,1)S(1)}, bf16[384,1024]{1,0:T(8,128)(2,1)}, u32[]{:S(2)}) copy-start(bf16[384,1024]{1,0:T(8,128)(2,1)} %up_ref.1) | copy-start | bytes 2359300
  0.6 164.7 %copy-start.1 = (bf16[384,1024]{1,0:T(8,128)(2,1)S(1)}, bf16[384,1024]{1,0:T(8,128)(2,1)}, u32[]{:S(2)}) copy-start(bf16[384,1024]{1,0:T(8,128)(2,1)} %gate_ref.1) | copy-start | bytes 2359300
  165.3 3.3 %copy-start.2 = (bf16[12,2,16,192]{3,2,1,0:T(8,128)(2,1)S(1)}, bf16[12,2,16,192]{3,2,1,0:T(8,128)(2,1)}, u32[]{:S(2)}) copy-start(bf16[12,2,16,192]{3,2,1,0:T(8,128)(2,1)} %get-tuple-element.6) | copy-start | bytes 442372
